TPU v7x, 32 devices: a whole 2x2x4 slice. The times are simulated.
32 devices in a mesh: task: 2 (over y), fsdp: 8 (over z, x), view: 2 (over core).
Axes of the slice: x: 2, y: 2, z: 4, core: 2. Of those that a mesh axis runs over, the one named last changes fastest.
Arguments:
- train_input: bfloat16 [4, 2048, 8192], P(('task', 'view'), 'fsdp'), parts along dimension 0, may hold values from -6 to 6
- train_query: bfloat16 [4, 2048, 4096], P(('task', 'view'), 'fsdp'), parts along dimension 0, may hold values from -120 to 120, as said below
- train_keys: bfloat16 [4, 2048, 512], P(('task', 'view'), 'fsdp'), parts along dimension 0, may hold values from -6 to 6, as said below
- train_target: bfloat16 [4, 2048, 4096], P(('task', 'view'), 'fsdp'), parts along dimension 0, may hold values from -6 to 6
- train_segments: int32 [4, 8, 256], P(('task', 'view'), 'fsdp'), parts along dimension 0, may hold values from 0 to 7, never falling along the last dimension, each value on 1 to 64 neighbouring positions
- value_weight: bfloat16 [8192, 512], P('fsdp'), may hold values from -0.0625 to 0.0625
- adapter_down: float32 [16384, 64], P(('task', 'fsdp')), parts along dimension 0, may hold values from -0.0625 to 0.0625
- adapter_up: float32 [128, 512], P('task'), parts along dimension 0, may hold values from -0.75 to 0.75
- score_input: bfloat16 [4, 512, 8192], P(('task', 'view'), 'fsdp'), parts along dimension 0, may hold values from -6 to 6
- score_query: bfloat16 [4, 512, 4096], P(('task', 'view'), 'fsdp'), parts along dimension 0, may hold values from -120 to 120, as said below
- score_keys: bfloat16 [4, 512, 512], P(('task', 'view'), 'fsdp'), parts along dimension 0, may hold values from -6 to 6, as said below
- score_segments: int32 [4, 8, 64], P(('task', 'view'), 'fsdp'), parts along dimension 0, may hold values from 0 to 3, never falling along the last dimension, each value on 1 to 32 neighbouring positions
Outputs:
- new_down: float32 [16384, 64], P(('task', 'fsdp')), parts along dimension 0
- new_up: float32 [128, 512], P('task'), parts along dimension 0
- scored: bfloat16 [4, 512, 4096], P(('task', 'view'), 'fsdp'), parts along dimension 0
There are 2 independent parts, one for each index of `task`. A program takes and returns all parts, laid end to end along the dimension named above; an argument that names none is the same for every part. Nothing has to cross between parts.
Inputs may be any that keep to these rules, and one draw needn't show every extreme that they name: `train_query`: query features of each token. `train_keys`: key features of each token. `score_query`: query features of each token. `score_keys`: key features of each token. `train_segments`: ids never decrease along a packed row. `score_segments`: ids never decrease along a packed row.
All inputs are finite; a program needn't handle non-finite values.
Results may differ from a plain program's by a relative error of at most 0.01.
Values may be sent and summed in bfloat16 or wider, within the bound.
A program may use at most 128 MiB of HBM per device.

v0:
```python
import jax
import jax.numpy as jnp
from jax import lax
from jax.experimental import pallas as pl
from jax.experimental.pallas import tpu as pltpu
from jax.sharding import PartitionSpec as P

Q_HEADS = 32
KV_HEADS = 4
HEAD_DIM = 128
GROUP = 8
VALUE_WIDTH = 512


adapter_scale_factor = 0.5
rate_down = 2e-05
rate_up = 0.001


def attend_row(query, keyset, value_rows, segment):
    length = query.shape[0]
    query_heads = query.reshape(length, KV_HEADS, GROUP, HEAD_DIM)
    key_heads = keyset.reshape(length, KV_HEADS, HEAD_DIM)
    logits = jnp.einsum(
        "qgjd,kgd->gjqk", query_heads, key_heads, preferred_element_type=jnp.float32
    ) * HEAD_DIM ** (-0.5)
    positions = jnp.arange(length, dtype=jnp.int32)
    allowed = (positions[None, :] <= positions[:, None]) & (segment[:, None] == segment[None, :])
    logits = jnp.where(allowed, logits, -1e30)
    peak = jnp.max(logits, axis=-1, keepdims=True)
    weights = jnp.exp(logits - peak)
    probs = (weights / jnp.sum(weights, axis=-1, keepdims=True)).astype(jnp.bfloat16)
    value_heads = value_rows.reshape(length, KV_HEADS, HEAD_DIM)
    attended = jnp.einsum("gjqk,kgd->qgjd", probs, value_heads, preferred_element_type=jnp.float32)
    return (probs, attended.reshape(length, Q_HEADS * HEAD_DIM))


def values_grad(probs, d_out):
    length = d_out.shape[0]
    heads = d_out.reshape(length, KV_HEADS, GROUP, HEAD_DIM)
    summed = jnp.einsum("gjqk,qgjd->kgd", probs, heads, preferred_element_type=jnp.float32)
    return summed.reshape(length, VALUE_WIDTH).astype(jnp.bfloat16)


def add_pieces(rows_in, pieces):
    return (
        jnp.dot(rows_in, pieces[0], preferred_element_type=jnp.float32),
        jnp.dot(rows_in, pieces[1], preferred_element_type=jnp.float32),
    )


def body(
    train_input,
    train_query,
    train_keys,
    train_target,
    train_segments,
    value_weight,
    adapter_down,
    adapter_up,
    score_input,
    score_query,
    score_keys,
    score_segments,
):
    width = train_input.shape[-1]
    value_width = value_weight.shape[1]
    count_rows = train_segments.shape[0] * train_segments.shape[1]
    row_length = train_segments.shape[2]
    score_length = score_segments.shape[2]
    down_half = adapter_down.astype(jnp.bfloat16)
    upper_weight_half = adapter_up.astype(jnp.bfloat16)
    train_rows = train_input.reshape(-1, width)
    frozen_base_weight, low = add_pieces(
        train_rows,
        (
            lax.all_gather(value_weight, "fsdp", axis=0, tiled=True),
            lax.all_gather(down_half, "fsdp", axis=0, tiled=True),
        ),
    )
    lower_rank_half = low.astype(jnp.bfloat16)
    value_rows = (
        frozen_base_weight
        + adapter_scale_factor
        * jnp.dot(lower_rank_half, upper_weight_half, preferred_element_type=jnp.float32)
    ).astype(jnp.bfloat16)
    probs, attended = jax.vmap(attend_row)(
        train_query,
        train_keys,
        value_rows.reshape(count_rows, row_length, -1),
        train_segments.reshape(count_rows, row_length),
    )
    d_out = (attended - train_target.astype(jnp.float32)).astype(jnp.bfloat16)
    value_output_gradient = jax.vmap(values_grad)(probs, d_out).reshape(-1, value_width)
    low_rank_gradient = (
        adapter_scale_factor
        * lax.dot_general(
            value_output_gradient,
            upper_weight_half,
            (((1,), (1,)), ((), ())),
            preferred_element_type=jnp.float32,
        )
    ).astype(jnp.bfloat16)
    local_up_gradient = adapter_scale_factor * lax.dot_general(
        lower_rank_half,
        value_output_gradient,
        (((0,), (0,)), ((), ())),
        preferred_element_type=jnp.float32,
    )
    grad_down = lax.psum_scatter(
        lax.dot_general(
            train_rows,
            low_rank_gradient,
            (((0,), (0,)), ((), ())),
            preferred_element_type=jnp.float32,
        ),
        "fsdp",
        scatter_dimension=0,
        tiled=True,
    )
    grad_down = lax.psum(grad_down, "view")
    up_weight_gradient = lax.psum(local_up_gradient, ("fsdp", "view"))
    new_down = adapter_down - rate_down * grad_down
    new_up = adapter_up - rate_up * up_weight_gradient
    new_down_half = new_down.astype(jnp.bfloat16)
    new_up_half = new_up.astype(jnp.bfloat16)
    score_rows = score_input.reshape(-1, width)
    score_base, score_low = add_pieces(
        score_rows,
        (
            lax.all_gather(value_weight, "fsdp", axis=0, tiled=True),
            lax.all_gather(new_down_half, "fsdp", axis=0, tiled=True),
        ),
    )
    score_values = (
        score_base
        + adapter_scale_factor
        * jnp.dot(score_low.astype(jnp.bfloat16), new_up_half, preferred_element_type=jnp.float32)
    ).astype(jnp.bfloat16)
    score_probs, score_attended = jax.vmap(attend_row)(
        score_query,
        score_keys,
        score_values.reshape(count_rows, score_length, -1),
        score_segments.reshape(count_rows, score_length),
    )
    scored = score_attended.astype(jnp.bfloat16)
    return (new_down, new_up, scored)


F32, BF16 = jnp.float32, jnp.bfloat16
N, DEPTH = 8, 4
BLOCK = 64
WINDOW = 2 * BLOCK
NT = (((1,), (1,)), ((), ()))
TN = (((0,), (0,)), ((), ()))
UP, DOWN, SIDE, TWIN, CORE = range(5)


def nt_dot(a, b):
    return lax.dot_general(a, b, NT, preferred_element_type=F32)


def tn_dot(a, b):
    return lax.dot_general(a, b, TN, preferred_element_type=F32)


def dot(a, b):
    return jnp.dot(a, b, preferred_element_type=F32)


def lanes(start, size):
    return pl.ds(pl.multiple_of(start, size), size)


def stack_heads(ref, rows, g):
    return jnp.concatenate(
        [ref[rows, lanes((g * GROUP + j) * HEAD_DIM, HEAD_DIM)] for j in range(GROUP)], axis=0
    )


def softmax_rows(logits, allowed):
    shape = logits.shape
    logits = (logits * HEAD_DIM ** (-0.5)).reshape(GROUP, BLOCK, shape[-1])
    logits = jnp.where(allowed[None], logits, -1e30)
    weights = jnp.exp(logits - jnp.max(logits, axis=-1, keepdims=True))
    probs = weights * (1.0 / jnp.sum(weights, axis=-1, keepdims=True))
    return probs.reshape(shape).astype(BF16)


def fused_kernel(
    x_hbm, q_hbm, k_hbm, goal_hbm, seg_hbm, w_hbm, down_hbm, up_hbm, sx_hbm, sq_hbm, sk_hbm, sseg_hbm,
    new_down_t, new_up, scored,
    xs, qs, ks, goal, seg, down_t, up_ref, sq, sk, sseg, seg_col, wbuf, dbuf, ndbuf, probs, sprobs, base, vals, dvals,
    low_s, slow_s, gmine, gsend, gpair, rsend, rrecv, fhalf, frecv, gu, gupair, gusum, gurecv, gupart, guall,
    s_loc, s_w, r_w, s_d, r_d, s_nd, r_nd, s_gp, r_gp, s_rs, r_rs, s_f, r_f,
    s_up, r_up, s_ur, r_ur, s_ua, r_ua, s_uc, r_uc,
):
    t, f, c = lax.axis_index("task"), lax.axis_index("fsdp"), lax.axis_index("view")
    z, x = lax.div(f, 2), lax.rem(f, 2)
    other_t, other_x, other_c = 1 - t, 1 - x, 1 - c
    width = xs.shape[1]
    part = width // N
    half = part // 2
    rows = vals.shape[0]
    late = []
    wcols = VALUE_WIDTH // 2

    def device(kind):
        return {
            UP: {"fsdp": f + 2},
            DOWN: {"fsdp": f - 2},
            SIDE: {"fsdp": 2 * z + other_x},
            TWIN: {"task": other_t},
            CORE: {"view": other_c},
        }[kind]

    def exists(kind):
        return {UP: z < DEPTH - 1, DOWN: z > 0}.get(kind, True)

    def start(make, pred=True):
        if pred is True:
            make().start()
        else:
            pl.when(pred)(lambda: make().start())
        late.append((make, pred))

    def send(kind, src, dst, s_sem, r_sem, pred=True):
        where = exists(kind)
        if where is not True:
            pred = where if pred is True else jnp.logical_and(where, pred)

        def make():
            return pltpu.make_async_remote_copy(
                src_ref=src, dst_ref=dst, send_sem=s_sem, recv_sem=r_sem,
                device_id=device(kind), device_id_type=pl.DeviceIdType.MESH,
            )

        start(make, pred)

    def peer_send(peer, src, dst, s_sem, r_sem):
        def make():
            return pltpu.make_async_remote_copy(
                src_ref=src, dst_ref=dst, send_sem=s_sem, recv_sem=r_sem,
                device_id={"fsdp": peer}, device_id_type=pl.DeviceIdType.MESH,
            )

        start(make)

    def arrived(dst, r_sem, pred=True):
        def wait():
            pltpu.make_async_remote_copy(
                src_ref=dst, dst_ref=dst, send_sem=r_sem, recv_sem=r_sem,
                device_id={"view": other_c}, device_id_type=pl.DeviceIdType.MESH,
            ).wait_recv()

        if pred is True:
            wait()
        else:
            pl.when(pred)(wait)

    def peers():
        return [lax.rem(f + k, N) for k in range(1, N)]

    barrier = pltpu.get_barrier_semaphore()
    for peer in peers():
        pl.semaphore_signal(barrier, inc=1, device_id={"fsdp": peer}, device_id_type=pl.DeviceIdType.MESH)
    for kind in (TWIN, CORE):
        pl.semaphore_signal(barrier, inc=1, device_id=device(kind), device_id_type=pl.DeviceIdType.MESH)

    local = [
        (down_hbm, down_t),
        (q_hbm, qs),
        (k_hbm, ks),
        (seg_hbm, seg),
        (sq_hbm, sq),
        (sk_hbm, sk),
        (sseg_hbm, sseg),
        (x_hbm, xs.at[pl.ds(0, rows)]),
        (sx_hbm, xs.at[pl.ds(rows, BLOCK)]),
        (up_hbm, up_ref),
        (goal_hbm, goal),
    ] + [(w_hbm.at[:, :, pl.ds(h * wcols, wcols)], wbuf.at[h, pl.ds(4 * f, 4)]) for h in range(2)]
    loads = [pltpu.make_async_copy(a, b, s_loc.at[i]) for i, (a, b) in enumerate(local)]
    for load in loads:
        load.start()
    loads[0].wait()
    for side in range(2):
        dbuf[2 * f + side] = down_t[:, side * half:(side + 1) * half].astype(BF16)
    pl.semaphore_wait(barrier, N + 1)

    line = [(d, s, z - s * d) for d in range(1, DEPTH) for s in (1, -1)]

    def inside(zp):
        return jnp.logical_and(zp >= 0, zp < DEPTH)

    def piece_send(buf, s_sem, r_sem, kind, i, pred=True):
        send(kind, buf.at[i], buf.at[i], s_sem.at[kind, i], r_sem.at[i], pred)

    def pieces_own(buf, s_sem, r_sem):
        for kind in (UP, DOWN, SIDE):
            piece_send(buf, s_sem, r_sem, kind, 2 * f + c)

    def pieces_line(buf, s_sem, r_sem, d):
        for dd, s, zp in line:
            if dd == d:
                ok, i = inside(zp), 2 * (2 * zp + x) + c
                arrived(buf.at[i], r_sem.at[i], ok)
                for kind in (UP if s > 0 else DOWN, SIDE, CORE):
                    piece_send(buf, s_sem, r_sem, kind, i, ok)

    def pieces_side(buf, s_sem, r_sem, d):
        for dd, s, zp in [(0, 1, z)] + line:
            if dd == d:
                ok, i = (True if d == 0 else inside(zp)), 2 * (2 * zp + other_x) + c
                arrived(buf.at[i], r_sem.at[i], ok)
                piece_send(buf, s_sem, r_sem, CORE, i, ok)

    def pieces_core(buf, r_sem):
        for peer in peers():
            i = 2 * peer + other_c
            arrived(buf.at[i], r_sem.at[i])

    mine, theirs = 2 * t + c, 2 * other_t + c

    def w_send(h, kind, i, pred=True):
        send(kind, wbuf.at[h, i], wbuf.at[h, i], s_w.at[h, kind, i], r_w.at[h, i], pred)

    def w_wait(h, i, pred=True):
        arrived(wbuf.at[h, i], r_w.at[h, i], pred)

    def w_own(h):
        for kind, q in ((UP, mine), (DOWN, mine), (SIDE, mine), (SIDE, theirs)):
            i = 4 * f + q
            src = w_hbm.at[q, :, pl.ds(h * wcols, wcols)]
            send(kind, src, wbuf.at[h, i], s_w.at[h, kind, i], r_w.at[h, i])

    def w_line(h, d):
        for dd, s, zp in line:
            if dd == d:
                ok, i = inside(zp), 4 * (2 * zp + x) + mine
                w_wait(h, i, ok)
                for kind in (UP if s > 0 else DOWN, SIDE, TWIN, CORE):
                    w_send(h, kind, i, ok)

    def w_side(h, d):
        if d == 0:
            i = 4 * (2 * z + other_x) + mine
            w_wait(h, i)
            w_send(h, CORE, i)
            i = 4 * (2 * z + other_x) + theirs
            w_wait(h, i)
            for kind in (UP, DOWN, CORE):
                w_send(h, kind, i)
            return
        for dd, s, zp in line:
            if dd == d:
                ok, i = inside(zp), 4 * (2 * zp + other_x) + mine
                w_wait(h, i, ok)
                if d > 1:
                    w_send(h, TWIN, i, ok)
                w_send(h, CORE, i, ok)

    def w_twin(h, d, xx):
        for dd, s, zp in line:
            if dd == d:
                ok, i = inside(zp), 4 * (2 * zp + xx) + theirs
                w_wait(h, i, ok)
                w_send(h, CORE, i, ok)

    def shards(d):
        if d == 0:
            return [(True, f), (True, 2 * z + other_x)]
        return [(inside(zp), 2 * zp + xx) for dd, s, zp in line if dd == d for xx in (x, other_x)]

    def run(pred, step):
        if pred is True:
            step()
        else:
            pl.when(pred)(step)

    def add_base(h, d):
        for n, (ok, shard) in enumerate(shards(d)):
            def step(n=n, shard=shard):
                if d or n:
                    for q in (2 * t + other_c, 2 * other_t + other_c):
                        w_wait(h, 4 * shard + q)
                weight = wbuf[h, pl.ds(4 * shard, 4)].reshape(part, wcols)
                base[:, h * wcols:(h + 1) * wcols] += dot(xs[:, lanes(shard * part, part)], weight)

            run(ok, step)

    def train_probs(b):
        first = max(b - 1, 0) * BLOCK
        position_q = b * BLOCK + lax.broadcasted_iota(jnp.int32, (BLOCK, WINDOW), 0)
        position_k = first + lax.broadcasted_iota(jnp.int32, (BLOCK, WINDOW), 1)
        same = seg_col[pl.ds(b * BLOCK, BLOCK), :] == seg[...].astype(F32)[:, first:first + WINDOW]
        allowed = (position_k <= position_q) & same

        def head_group(g, _):
            q = stack_heads(qs, pl.ds(b * BLOCK, BLOCK), g)
            k = ks[pl.ds(first, WINDOW), lanes(g * HEAD_DIM, HEAD_DIM)]
            probs[b * KV_HEADS + g] = softmax_rows(nt_dot(q, k), allowed)
            return 0

        lax.fori_loop(0, KV_HEADS, head_group, 0)

    def score_probs():
        order_q = lax.broadcasted_iota(jnp.int32, (BLOCK, BLOCK), 0)
        order_k = lax.broadcasted_iota(jnp.int32, (BLOCK, BLOCK), 1)
        ids = sseg[...].astype(F32)
        column = jnp.broadcast_to(jnp.concatenate([ids, ids], axis=1), (WINDOW, WINDOW)).T
        allowed = (order_k <= order_q) & (column[:BLOCK, :BLOCK] == ids)

        def head_group(g, _):
            q = stack_heads(sq, pl.ds(0, BLOCK), g)
            sprobs[g] = softmax_rows(nt_dot(q, sk[:, lanes(g * HEAD_DIM, HEAD_DIM)]), allowed)
            return 0

        lax.fori_loop(0, KV_HEADS, head_group, 0)

    def low_step(i, acc):
        return acc + nt_dot(xs[pl.ds(0, rows), lanes(i * half, half)], dbuf[i])

    def attention(h):
        halves = pl.ds(h * wcols, wcols)
        up_half = up_ref[:, halves].astype(BF16)
        mixed = adapter_scale_factor * dot(low_s[...], up_half)
        vals[:, halves] = (base[pl.ds(0, rows), halves] + mixed).astype(BF16)
        for b in range(rows // BLOCK):
            first = max(b - 1, 0) * BLOCK

            def head_group(g, _, b=b, first=first):
                p = probs[b * KV_HEADS + g]
                cols = lanes(g * HEAD_DIM, HEAD_DIM)
                attended = dot(p, vals[pl.ds(first, WINDOW), cols])
                d_out = (attended - stack_heads(goal, pl.ds(b * BLOCK, BLOCK), g).astype(F32)).astype(BF16)
                dvals[pl.ds(first, WINDOW), cols] += tn_dot(p, d_out)
                return 0

            lax.fori_loop(h * KV_HEADS // 2, (h + 1) * KV_HEADS // 2, head_group, 0)

    dset = (dbuf, s_d, r_d)
    pieces_own(*dset)
    w_own(0)
    base[...] = jnp.zeros_like(base)
    dvals[...] = jnp.zeros_like(dvals)
    for i in range(1, 4):
        loads[i].wait()
    seg_col[...] = jnp.broadcast_to(seg[...].astype(F32), (WINDOW, rows)).T
    train_probs(0)
    pieces_line(*dset, 1)
    w_line(0, 1)
    pieces_side(*dset, 0)
    w_side(0, 0)
    w_own(1)
    train_probs(1)
    pieces_line(*dset, 2)
    w_line(0, 2)
    pieces_side(*dset, 1)
    w_side(0, 1)
    w_twin(0, 1, x)
    w_twin(0, 1, other_x)
    train_probs(2)
    pieces_line(*dset, 3)
    w_line(0, 3)
    pieces_side(*dset, 2)
    w_side(0, 2)
    w_twin(0, 2, x)
    w_line(1, 1)
    w_side(1, 0)
    train_probs(3)
    pieces_side(*dset, 3)
    w_side(0, 3)
    w_twin(0, 2, other_x)
    w_twin(0, 3, x)
    w_line(1, 2)
    w_side(1, 1)
    for i in range(4, len(loads)):
        loads[i].wait()
    score_probs()
    w_twin(1, 1, x)
    w_twin(1, 1, other_x)
    w_line(1, 3)
    w_twin(0, 3, other_x)
    pieces_core(dbuf, r_d)
    low = lax.fori_loop(0, 2 * N, low_step, jnp.zeros((rows, low_s.shape[1]), F32)).astype(BF16)
    low_s[...] = low
    w_side(1, 2)
    w_twin(1, 2, x)
    for d in range(DEPTH):
        add_base(0, d)
    w_side(1, 3)
    w_twin(1, 2, other_x)
    w_twin(1, 3, x)
    attention(0)
    w_twin(1, 3, other_x)
    for d in range(DEPTH):
        add_base(1, d)
    attention(1)
    up_half = up_ref[...].astype(BF16)
    dv = dvals[...].astype(BF16)
    dlow_t = (adapter_scale_factor * nt_dot(up_half, dv)).astype(BF16)

    def grad_of(peer, side):
        return dot(dlow_t, xs[pl.ds(0, rows), lanes(peer * part + side * half, half)])

    order = peers() + [f]
    for n, peer in enumerate(order):
        gsend[n] = grad_of(peer, other_c).astype(BF16)
        send(CORE, gsend.at[n], gpair.at[n], s_gp.at[n], r_gp.at[n])
    gu[...] = adapter_scale_factor * tn_dot(low_s[...], dv)
    ucols = VALUE_WIDTH // 2
    send(CORE, gu.at[:, lanes(other_c * ucols, ucols)], gupair, s_up, r_up)
    for n, peer in enumerate(order[:-1]):
        gmine[n] = grad_of(peer, c)
        arrived(gpair.at[n], r_gp.at[n])
        rsend[n] = (gmine[n] + gpair[n].astype(F32)).astype(BF16)
        peer_send(peer, rsend.at[n], rrecv.at[n], s_rs.at[n], r_rs.at[n])
    arrived(gupair, r_up)
    gusum[...] = gu[:, lanes(c * ucols, ucols)] + gupair[...]
    urows = gusum.shape[0] // N
    for n, peer in enumerate(order[:-1]):
        peer_send(
            peer, gusum.at[pl.ds(pl.multiple_of(peer * urows, urows), urows)], gurecv.at[n], s_ur.at[n], r_ur.at[n]
        )
    gmine[N - 1] = grad_of(f, c)
    arrived(gpair.at[N - 1], r_gp.at[N - 1])
    total = gmine[N - 1] + gpair[N - 1].astype(F32)
    for n in range(N - 1):
        arrived(rrecv.at[n], r_rs.at[n])
        total = total + rrecv[n].astype(F32)
    new_half = down_t[:, lanes(c * half, half)] - rate_down * total
    fhalf[...] = new_half
    ndbuf[2 * f + c] = new_half.astype(BF16)
    ndset = (ndbuf, s_nd, r_nd)
    pieces_own(*ndset)
    send(CORE, fhalf, frecv, s_f, r_f)

    utotal = gusum[pl.ds(pl.multiple_of(f * urows, urows), urows), :]
    for n in range(N - 1):
        arrived(gurecv.at[n], r_ur.at[n])
        utotal = utotal + gurecv[n]
    gupart[...] = utotal
    guall[c, pl.ds(pl.multiple_of(f * urows, urows), urows), :] = utotal
    for n, peer in enumerate(order[:-1]):
        peer_send(
            peer, gupart, guall.at[c, pl.ds(pl.multiple_of(f * urows, urows), urows)], s_ua.at[n], r_ua.at[f]
        )
    slow_s[...] = jnp.zeros_like(slow_s)

    def add_slow(d):
        for n, (ok, shard) in enumerate(shards(d)):
            def step(n=n, shard=shard):
                if d or n:
                    i = 2 * shard + other_c
                    arrived(ndbuf.at[i], r_nd.at[i])
                acc = slow_s[...]
                for side in range(2):
                    cols = lanes(shard * part + side * half, half)
                    acc = acc + nt_dot(xs[pl.ds(rows, BLOCK), cols], ndbuf[2 * shard + side])
                slow_s[...] = acc

            run(ok, step)

    pieces_line(*ndset, 1)
    pieces_side(*ndset, 0)
    pieces_line(*ndset, 2)
    pieces_side(*ndset, 1)
    arrived(frecv, r_f)
    new_down_t[:, lanes(c * half, half)] = fhalf[...]
    new_down_t[:, lanes(other_c * half, half)] = frecv[...]
    ndbuf[2 * f + other_c] = frecv[...].astype(BF16)
    add_slow(0)
    pieces_line(*ndset, 3)
    pieces_side(*ndset, 2)
    for peer in peers():
        arrived(guall.at[c, pl.ds(pl.multiple_of(peer * urows, urows), urows)], r_ua.at[peer])
    send(CORE, guall.at[c], guall.at[c], s_uc, r_uc)
    add_slow(1)
    pieces_side(*ndset, 3)
    arrived(guall.at[other_c], r_uc)
    for side in range(2):
        cols = pl.ds(side * ucols, ucols)
        new_up[:, cols] = up_ref[:, cols] - rate_up * guall[side]
    add_slow(2)
    add_slow(3)
    slow = slow_s[...].astype(BF16)
    svals = (
        base[pl.ds(rows, BLOCK), :] + adapter_scale_factor * dot(slow, new_up[...].astype(BF16))
    ).astype(BF16)
    for g in range(KV_HEADS):
        attended = dot(sprobs[g], svals[:, g * HEAD_DIM:(g + 1) * HEAD_DIM]).astype(BF16)
        for j in range(GROUP):
            at = (g * GROUP + j) * HEAD_DIM
            scored[:, at:at + HEAD_DIM] = attended[j * BLOCK:(j + 1) * BLOCK]

    def finish(make):
        make().wait_send()

    for make, pred in late:
        if pred is True:
            finish(make)
        else:
            pl.when(pred)(lambda make=make: finish(make))


def fused_body(
    train_input, train_query, train_keys, train_target, train_segments, value_weight, adapter_down, adapter_up,
    score_input, score_query, score_keys, score_segments,
):
    rows, width = train_input.shape[1:]
    part, rank = adapter_down.shape
    half = part // 2
    heads = train_query.shape[2]
    srows = score_input.shape[1]
    vw = value_weight.shape[1]
    hbm, vmem = pl.BlockSpec(memory_space=pl.ANY), pl.BlockSpec(memory_space=pltpu.VMEM)
    sem = pltpu.SemaphoreType.DMA
    uc, ur = vw // 2, rank // N
    scratch = [
        pltpu.VMEM((rows + srows, width), BF16),
        pltpu.VMEM((rows, heads), BF16),
        pltpu.VMEM((rows, vw), BF16),
        pltpu.VMEM((rows, heads), BF16),
        pltpu.VMEM((1, rows), jnp.int32),
        pltpu.VMEM((rank, part), F32),
        pltpu.VMEM((rank, vw), F32),
        pltpu.VMEM((srows, heads), BF16),
        pltpu.VMEM((srows, vw), BF16),
        pltpu.VMEM((1, srows), jnp.int32),
        pltpu.VMEM((rows, WINDOW), F32),
        pltpu.VMEM((2, 4 * N, part // 4, vw // 2), BF16),
        pltpu.VMEM((2 * N, rank, half), BF16),
        pltpu.VMEM((2 * N, rank, half), BF16),
        pltpu.VMEM((rows // BLOCK * KV_HEADS, GROUP * BLOCK, WINDOW), BF16),
        pltpu.VMEM((KV_HEADS, GROUP * BLOCK, BLOCK), BF16),
        pltpu.VMEM((rows + srows, vw), F32),
        pltpu.VMEM((rows, vw), BF16),
        pltpu.VMEM((rows, vw), F32),
        pltpu.VMEM((rows, rank), BF16),
        pltpu.VMEM((srows, rank), F32),
        pltpu.VMEM((N, rank, half), F32),
        pltpu.VMEM((N, rank, half), BF16),
        pltpu.VMEM((N, rank, half), BF16),
        pltpu.VMEM((N - 1, rank, half), BF16),
        pltpu.VMEM((N - 1, rank, half), BF16),
        pltpu.VMEM((rank, half), F32),
        pltpu.VMEM((rank, half), F32),
        pltpu.VMEM((rank, vw), F32),
        pltpu.VMEM((rank, uc), F32),
        pltpu.VMEM((rank, uc), F32),
        pltpu.VMEM((N - 1, ur, uc), F32),
        pltpu.VMEM((ur, uc), F32),
        pltpu.VMEM((2, rank, uc), F32),
        sem((13,)),
        sem((2, 5, 4 * N)), sem((2, 4 * N)),
        sem((5, 2 * N)), sem((2 * N,)),
        sem((5, 2 * N)), sem((2 * N,)),
        sem((N,)), sem((N,)),
        sem((N - 1,)), sem((N - 1,)),
        sem, sem,
        sem, sem,
        sem((N - 1,)), sem((N - 1,)),
        sem((N - 1,)), sem((N,)),
        sem, sem,
    ]
    new_down_t, new_up, scored = pl.pallas_call(
        fused_kernel,
        out_shape=(
            jax.ShapeDtypeStruct((rank, part), F32),
            jax.ShapeDtypeStruct(adapter_up.shape, F32),
            jax.ShapeDtypeStruct((srows, heads), BF16),
        ),
        in_specs=[hbm] * 12,
        out_specs=(vmem, vmem, vmem),
        scratch_shapes=scratch,
        compiler_params=pltpu.CompilerParams(
            collective_id=0, has_side_effects=True, vmem_limit_bytes=63 * 1024 * 1024
        ),
        name="test_time_step",
    )(
        train_input[0], train_query[0], train_keys[0], train_target[0], train_segments.reshape(1, rows),
        value_weight.reshape(4, part // 4, vw), adapter_down.T, adapter_up,
        score_input[0], score_query[0], score_keys[0], score_segments.reshape(1, srows),
    )
    return (new_down_t.T, new_up, scored[None])


def solution(mesh):
    in_specs = (
        P(("task", "view"), "fsdp", None),
        P(("task", "view"), "fsdp", None),
        P(("task", "view"), "fsdp", None),
        P(("task", "view"), "fsdp", None),
        P(("task", "view"), "fsdp", None),
        P("fsdp", None),
        P(("task", "fsdp"), None),
        P("task", None),
        P(("task", "view"), "fsdp", None),
        P(("task", "view"), "fsdp", None),
        P(("task", "view"), "fsdp", None),
        P(("task", "view"), "fsdp", None),
    )
    out_specs = (P(("task", "fsdp"), None), P("task", None), P(("task", "view"), "fsdp", None))
    local = fused_body if (mesh.shape["fsdp"], mesh.shape["view"]) == (8, 2) else body
    return jax.shard_map(local, mesh=mesh, in_specs=in_specs, out_specs=out_specs, check_vma=False)
```

profile of v0, /device:TPU:1, one launch (start us, length us, event | category | flops | bytes accessed | tf_op | source)
XLA Modules:
  0.0 105.3 jit_solution(8718266635220377932)
XLA Ops:
  0.6 99.6 %test_time_step.1 = (f32[64,1024]{1,0:T(8,128)}, f32[64,512]{1,0:T(8,128)}, bf16[64,4096]{1,0:T(8,128)(2,1)}) custom-call(bf16[256,8192]{1,0:T(8,128)(2,1)} %bitcast.13, bf16[256,4096]{1,0:T(8,128)(2,1)} %bitcast.14, bf16[256,512]{1,0:T(8,128)(2,1)} %bitcast.20, bf16[256,4096]{1,0:T(8,128)(2,1)} %bitcast.15, s32[1,256]{1,0:T(1,128)} %bitcast.24, ...), custom_call_target="tpu_custom_call" | custom-call | tf_op jit(solution)/shard_map/test_time_step/pallas_call | solution.py:667
  100.2 1.7 %copy.18 = f32[1024,64]{0,1:T(8,128)} copy(f32[1024,64]{0,1:T(8,128)} %bitcast.22) | data formatting | bytes 524288
  101.9 1.6 %copy.19 = f32[64,512]{1,0:T(8,128)} copy(f32[64,512]{1,0:T(8,128)} %get-tuple-element.13) | data formatting | bytes 262144
  103.5 1.9 %copy.20 = bf16[1,64,4096]{2,1,0:T(8,128)(2,1)} copy(bf16[1,64,4096]{2,1,0:T(8,128)(2,1)} %bitcast.19) | data formatting | bytes 1048576
where the time goes:
time: 106 us; the launch traced here: 105 us
  Pallas kernels  99.6 us (94%)
  local copies, waits for them, and re-layouts  5.11 us (5%)
    pallas_call x1, Pallas kernels, fused_body(): pl.pallas_call(fused_kernel, out_shape=(jax.ShapeDtypeStruct((rank, part)...  99.6 us
    unnamed x3, local copies, waits for them, and re-layouts  5.11 us

commit v1 on v0

--- a/solution.py
+++ b/solution.py
@@ -191,9 +191,10 @@
     x_hbm, q_hbm, k_hbm, goal_hbm, seg_hbm, w_hbm, down_hbm, up_hbm, sx_hbm, sq_hbm, sk_hbm, sseg_hbm,
     new_down_t, new_up, scored,
     xs, qs, ks, goal, seg, down_t, up_ref, sq, sk, sseg, seg_col, wbuf, dbuf, ndbuf, probs, sprobs, base, vals, dvals,
-    low_s, slow_s, gmine, gsend, gpair, rsend, rrecv, fhalf, frecv, gu, gupair, gusum, gurecv, gupart, guall,
-    s_loc, s_w, r_w, s_d, r_d, s_nd, r_nd, s_gp, r_gp, s_rs, r_rs, s_f, r_f,
-    s_up, r_up, s_ur, r_ur, s_ua, r_ua, s_uc, r_uc,
+    low_s, slow_s, slow_recv, gsend, gpair, rsend, rside, rline, rrecv, fhalf, frecv,
+    gu, gupair, gusum, guside, guline, guall,
+    s_loc, s_w, r_w, s_wc, r_wc, s_d, r_d, s_nd, r_nd, s_gp, r_gp, s_rx, r_rx, s_rs, r_rs, s_f, r_f,
+    s_up, r_up, s_ur, r_ur, s_ua, r_ua, s_uc, r_uc, s_sx, r_sx, s_sl, r_sl,
 ):
     t, f, c = lax.axis_index("task"), lax.axis_index("fsdp"), lax.axis_index("view")
     z, x = lax.div(f, 2), lax.rem(f, 2)
@@ -257,6 +258,17 @@
             wait()
         else:
             pl.when(pred)(wait)
+
+    def flush():
+        def finish(make):
+            make().wait_send()
+
+        for make, pred in late:
+            if pred is True:
+                finish(make)
+            else:
+                pl.when(pred)(lambda make=make: finish(make))
+        late.clear()
 
     def peers():
         return [lax.rem(f + k, N) for k in range(1, N)]
@@ -320,13 +332,17 @@
             i = 2 * peer + other_c
             arrived(buf.at[i], r_sem.at[i])
 
-    mine, theirs = 2 * t + c, 2 * other_t + c
+    mine, theirs = 2 * c + t, 2 * c + other_t
 
     def w_send(h, kind, i, pred=True):
         send(kind, wbuf.at[h, i], wbuf.at[h, i], s_w.at[h, kind, i], r_w.at[h, i], pred)
 
     def w_wait(h, i, pred=True):
         arrived(wbuf.at[h, i], r_w.at[h, i], pred)
+
+    def w_core(h, shard, pred=True):
+        pair = wbuf.at[h, pl.ds(4 * shard + 2 * c, 2)]
+        send(CORE, pair, pair, s_wc.at[h, shard], r_wc.at[h, shard], pred)
 
     def w_own(h):
         for kind, q in ((UP, mine), (DOWN, mine), (SIDE, mine), (SIDE, theirs)):
@@ -339,18 +355,18 @@
             if dd == d:
                 ok, i = inside(zp), 4 * (2 * zp + x) + mine
                 w_wait(h, i, ok)
-                for kind in (UP if s > 0 else DOWN, SIDE, TWIN, CORE):
+                for kind in (UP if s > 0 else DOWN, SIDE, TWIN):
                     w_send(h, kind, i, ok)
 
     def w_side(h, d):
         if d == 0:
             i = 4 * (2 * z + other_x) + mine
             w_wait(h, i)
-            w_send(h, CORE, i)
             i = 4 * (2 * z + other_x) + theirs
             w_wait(h, i)
-            for kind in (UP, DOWN, CORE):
+            for kind in (UP, DOWN):
                 w_send(h, kind, i)
+            w_core(h, 2 * z + other_x)
             return
         for dd, s, zp in line:
             if dd == d:
@@ -358,14 +374,13 @@
                 w_wait(h, i, ok)
                 if d > 1:
                     w_send(h, TWIN, i, ok)
-                w_send(h, CORE, i, ok)
 
     def w_twin(h, d, xx):
         for dd, s, zp in line:
             if dd == d:
                 ok, i = inside(zp), 4 * (2 * zp + xx) + theirs
                 w_wait(h, i, ok)
-                w_send(h, CORE, i, ok)
+                w_core(h, 2 * zp + xx, ok)
 
     def shards(d):
         if d == 0:
@@ -382,10 +397,10 @@
         for n, (ok, shard) in enumerate(shards(d)):
             def step(n=n, shard=shard):
                 if d or n:
-                    for q in (2 * t + other_c, 2 * other_t + other_c):
-                        w_wait(h, 4 * shard + q)
+                    arrived(wbuf.at[h, pl.ds(4 * shard + 2 * other_c, 2)], r_wc.at[h, shard])
                 weight = wbuf[h, pl.ds(4 * shard, 4)].reshape(part, wcols)
-                base[:, h * wcols:(h + 1) * wcols] += dot(xs[:, lanes(shard * part, part)], weight)
+                both = xs[pl.ds(0, rows + BLOCK), lanes(shard * part, part)]
+                base[:, h * wcols:(h + 1) * wcols] += dot(both, weight)
 
             run(ok, step)
 
@@ -439,6 +454,7 @@
 
             lax.fori_loop(h * KV_HEADS // 2, (h + 1) * KV_HEADS // 2, head_group, 0)
 
+    sx_other = xs.at[pl.ds(rows + BLOCK, BLOCK)]
     dset = (dbuf, s_d, r_d)
     pieces_own(*dset)
     w_own(0)
@@ -453,6 +469,7 @@
     pieces_side(*dset, 0)
     w_side(0, 0)
     w_own(1)
+    send(CORE, sx_hbm, sx_other, s_sx, r_sx)
     train_probs(1)
     pieces_line(*dset, 2)
     w_line(0, 2)
@@ -504,87 +521,82 @@
     def grad_of(peer, side):
         return dot(dlow_t, xs[pl.ds(0, rows), lanes(peer * part + side * half, half)])
 
-    order = peers() + [f]
+    turns = [lax.rem(z + k, DEPTH) for k in range(1, DEPTH)] + [z]
+    order = [2 * zt + xx for zt in turns for xx in (other_x, x)]
     for n, peer in enumerate(order):
         gsend[n] = grad_of(peer, other_c).astype(BF16)
         send(CORE, gsend.at[n], gpair.at[n], s_gp.at[n], r_gp.at[n])
     gu[...] = adapter_scale_factor * tn_dot(low_s[...], dv)
     ucols = VALUE_WIDTH // 2
     send(CORE, gu.at[:, lanes(other_c * ucols, ucols)], gupair, s_up, r_up)
-    for n, peer in enumerate(order[:-1]):
-        gmine[n] = grad_of(peer, c)
+
+    def core_sum(n):
+        mine_of = grad_of(order[n], c)
         arrived(gpair.at[n], r_gp.at[n])
-        rsend[n] = (gmine[n] + gpair[n].astype(F32)).astype(BF16)
-        peer_send(peer, rsend.at[n], rrecv.at[n], s_rs.at[n], r_rs.at[n])
+        return mine_of + gpair[n].astype(F32)
+
+    for k in range(DEPTH):
+        rsend[k] = core_sum(2 * k).astype(BF16)
+        send(SIDE, rsend.at[k], rside.at[k], s_rx.at[k], r_rx.at[k])
     arrived(gupair, r_up)
     gusum[...] = gu[:, lanes(c * ucols, ucols)] + gupair[...]
-    urows = gusum.shape[0] // N
-    for n, peer in enumerate(order[:-1]):
-        peer_send(
-            peer, gusum.at[pl.ds(pl.multiple_of(peer * urows, urows), urows)], gurecv.at[n], s_ur.at[n], r_ur.at[n]
-        )
-    gmine[N - 1] = grad_of(f, c)
-    arrived(gpair.at[N - 1], r_gp.at[N - 1])
-    total = gmine[N - 1] + gpair[N - 1].astype(F32)
-    for n in range(N - 1):
-        arrived(rrecv.at[n], r_rs.at[n])
-        total = total + rrecv[n].astype(F32)
+    send(SIDE, gusum, guside, s_ur, r_ur)
+    for k in range(DEPTH):
+        total = core_sum(2 * k + 1)
+        arrived(rside.at[k], r_rx.at[k])
+        total = total + rside[k].astype(F32)
+        if k < DEPTH - 1:
+            rline[k] = total.astype(BF16)
+            peer_send(2 * turns[k] + x, rline.at[k], rrecv.at[k], s_rs.at[k], r_rs.at[k])
+    arrived(guside, r_ur)
+    guline[z] = (gusum[...] + guside[...]).astype(BF16)
+    flush()
+    for k in range(DEPTH - 1):
+        arrived(rrecv.at[k], r_rs.at[k])
+        total = total + rrecv[k].astype(F32)
     new_half = down_t[:, lanes(c * half, half)] - rate_down * total
+    ndbuf[f] = new_half.astype(BF16)
+    for k in range(DEPTH - 1):
+        peer_send(2 * turns[k] + x, ndbuf.at[f], ndbuf.at[f], s_nd.at[k], r_nd.at[f])
+    send(SIDE, ndbuf.at[f], ndbuf.at[f], s_nd.at[DEPTH - 1], r_nd.at[f])
+    for k in range(DEPTH - 1):
+        peer_send(2 * turns[k] + x, guline.at[z], guline.at[z], s_ua.at[k], r_ua.at[z])
     fhalf[...] = new_half
-    ndbuf[2 * f + c] = new_half.astype(BF16)
-    ndset = (ndbuf, s_nd, r_nd)
-    pieces_own(*ndset)
     send(CORE, fhalf, frecv, s_f, r_f)
 
-    utotal = gusum[pl.ds(pl.multiple_of(f * urows, urows), urows), :]
-    for n in range(N - 1):
-        arrived(gurecv.at[n], r_ur.at[n])
-        utotal = utotal + gurecv[n]
-    gupart[...] = utotal
-    guall[c, pl.ds(pl.multiple_of(f * urows, urows), urows), :] = utotal
-    for n, peer in enumerate(order[:-1]):
-        peer_send(
-            peer, gupart, guall.at[c, pl.ds(pl.multiple_of(f * urows, urows), urows)], s_ua.at[n], r_ua.at[f]
-        )
-    slow_s[...] = jnp.zeros_like(slow_s)
-
-    def add_slow(d):
-        for n, (ok, shard) in enumerate(shards(d)):
-            def step(n=n, shard=shard):
-                if d or n:
-                    i = 2 * shard + other_c
-                    arrived(ndbuf.at[i], r_nd.at[i])
-                acc = slow_s[...]
-                for side in range(2):
-                    cols = lanes(shard * part + side * half, half)
-                    acc = acc + nt_dot(xs[pl.ds(rows, BLOCK), cols], ndbuf[2 * shard + side])
-                slow_s[...] = acc
-
-            run(ok, step)
-
-    pieces_line(*ndset, 1)
-    pieces_side(*ndset, 0)
-    pieces_line(*ndset, 2)
-    pieces_side(*ndset, 1)
+    def slow_of(shard):
+        cols = lanes(shard * part + c * half, half)
+        return nt_dot(xs[pl.ds(rows, 2 * BLOCK), cols], ndbuf[shard])
+
+    arrived(sx_other, r_sx)
+    slow = slow_of(f)
+    for k in range(DEPTH - 1):
+        shard = 2 * turns[k] + x
+        arrived(ndbuf.at[shard], r_nd.at[shard])
+        send(SIDE, ndbuf.at[shard], ndbuf.at[shard], s_nd.at[DEPTH + k], r_nd.at[shard])
+    for k in range(DEPTH - 1):
+        slow = slow + slow_of(2 * turns[k] + x)
+        arrived(guline.at[turns[k]], r_ua.at[turns[k]])
+    utotal = guline[0].astype(F32)
+    for k in range(1, DEPTH):
+        utotal = utotal + guline[k].astype(F32)
+    guall[c] = utotal
+    send(CORE, guall.at[c], guall.at[c], s_uc, r_uc)
     arrived(frecv, r_f)
     new_down_t[:, lanes(c * half, half)] = fhalf[...]
     new_down_t[:, lanes(other_c * half, half)] = frecv[...]
-    ndbuf[2 * f + other_c] = frecv[...].astype(BF16)
-    add_slow(0)
-    pieces_line(*ndset, 3)
-    pieces_side(*ndset, 2)
-    for peer in peers():
-        arrived(guall.at[c, pl.ds(pl.multiple_of(peer * urows, urows), urows)], r_ua.at[peer])
-    send(CORE, guall.at[c], guall.at[c], s_uc, r_uc)
-    add_slow(1)
-    pieces_side(*ndset, 3)
+    for zt in [z] + turns[:-1]:
+        shard = 2 * zt + other_x
+        arrived(ndbuf.at[shard], r_nd.at[shard])
+        slow = slow + slow_of(shard)
+    slow_s[...] = slow
+    send(CORE, slow_s.at[pl.ds(BLOCK, BLOCK)], slow_recv, s_sl, r_sl)
     arrived(guall.at[other_c], r_uc)
     for side in range(2):
         cols = pl.ds(side * ucols, ucols)
         new_up[:, cols] = up_ref[:, cols] - rate_up * guall[side]
-    add_slow(2)
-    add_slow(3)
-    slow = slow_s[...].astype(BF16)
+    arrived(slow_recv, r_sl)
+    slow = (slow_s[pl.ds(0, BLOCK), :] + slow_recv[...]).astype(BF16)
     svals = (
         base[pl.ds(rows, BLOCK), :] + adapter_scale_factor * dot(slow, new_up[...].astype(BF16))
     ).astype(BF16)
@@ -594,14 +606,7 @@
             at = (g * GROUP + j) * HEAD_DIM
             scored[:, at:at + HEAD_DIM] = attended[j * BLOCK:(j + 1) * BLOCK]
 
-    def finish(make):
-        make().wait_send()
-
-    for make, pred in late:
-        if pred is True:
-            finish(make)
-        else:
-            pl.when(pred)(lambda make=make: finish(make))
+    flush()
 
 
 def fused_body(
@@ -614,11 +619,12 @@
     heads = train_query.shape[2]
     srows = score_input.shape[1]
     vw = value_weight.shape[1]
-    hbm, vmem = pl.BlockSpec(memory_space=pl.ANY), pl.BlockSpec(memory_space=pltpu.VMEM)
+    hbm, vmem = pl.BlockSpec(memory_space=pltpu.HBM), pl.BlockSpec(memory_space=pltpu.VMEM)
     sem = pltpu.SemaphoreType.DMA
-    uc, ur = vw // 2, rank // N
+    uc = vw // 2
+    piece = (rank, half)
     scratch = [
-        pltpu.VMEM((rows + srows, width), BF16),
+        pltpu.VMEM((rows + 2 * srows, width), BF16),
         pltpu.VMEM((rows, heads), BF16),
         pltpu.VMEM((rows, vw), BF16),
         pltpu.VMEM((rows, heads), BF16),
@@ -630,38 +636,44 @@
         pltpu.VMEM((1, srows), jnp.int32),
         pltpu.VMEM((rows, WINDOW), F32),
         pltpu.VMEM((2, 4 * N, part // 4, vw // 2), BF16),
-        pltpu.VMEM((2 * N, rank, half), BF16),
-        pltpu.VMEM((2 * N, rank, half), BF16),
+        pltpu.VMEM((2 * N, *piece), BF16),
+        pltpu.VMEM((N, *piece), BF16),
         pltpu.VMEM((rows // BLOCK * KV_HEADS, GROUP * BLOCK, WINDOW), BF16),
         pltpu.VMEM((KV_HEADS, GROUP * BLOCK, BLOCK), BF16),
         pltpu.VMEM((rows + srows, vw), F32),
         pltpu.VMEM((rows, vw), BF16),
         pltpu.VMEM((rows, vw), F32),
         pltpu.VMEM((rows, rank), BF16),
+        pltpu.VMEM((2 * srows, rank), F32),
         pltpu.VMEM((srows, rank), F32),
-        pltpu.VMEM((N, rank, half), F32),
-        pltpu.VMEM((N, rank, half), BF16),
-        pltpu.VMEM((N, rank, half), BF16),
-        pltpu.VMEM((N - 1, rank, half), BF16),
-        pltpu.VMEM((N - 1, rank, half), BF16),
-        pltpu.VMEM((rank, half), F32),
-        pltpu.VMEM((rank, half), F32),
+        pltpu.VMEM((N, *piece), BF16),
+        pltpu.VMEM((N, *piece), BF16),
+        pltpu.VMEM((DEPTH, *piece), BF16),
+        pltpu.VMEM((DEPTH, *piece), BF16),
+        pltpu.VMEM((DEPTH - 1, *piece), BF16),
+        pltpu.VMEM((DEPTH - 1, *piece), BF16),
+        pltpu.VMEM(piece, F32),
+        pltpu.VMEM(piece, F32),
         pltpu.VMEM((rank, vw), F32),
         pltpu.VMEM((rank, uc), F32),
         pltpu.VMEM((rank, uc), F32),
-        pltpu.VMEM((N - 1, ur, uc), F32),
-        pltpu.VMEM((ur, uc), F32),
+        pltpu.VMEM((rank, uc), F32),
+        pltpu.VMEM((DEPTH, rank, uc), BF16),
         pltpu.VMEM((2, rank, uc), F32),
         sem((13,)),
         sem((2, 5, 4 * N)), sem((2, 4 * N)),
+        sem((2, N)), sem((2, N)),
         sem((5, 2 * N)), sem((2 * N,)),
-        sem((5, 2 * N)), sem((2 * N,)),
+        sem((2 * DEPTH - 1,)), sem((N,)),
         sem((N,)), sem((N,)),
-        sem((N - 1,)), sem((N - 1,)),
+        sem((DEPTH,)), sem((DEPTH,)),
+        sem((DEPTH - 1,)), sem((DEPTH - 1,)),
         sem, sem,
         sem, sem,
-        sem((N - 1,)), sem((N - 1,)),
-        sem((N - 1,)), sem((N,)),
+        sem, sem,
+        sem((DEPTH - 1,)), sem((DEPTH,)),
+        sem, sem,
+        sem, sem,
         sem, sem,
     ]
     new_down_t, new_up, scored = pl.pallas_call(
@@ -675,7 +687,7 @@
         out_specs=(vmem, vmem, vmem),
         scratch_shapes=scratch,
         compiler_params=pltpu.CompilerParams(
-            collective_id=0, has_side_effects=True, vmem_limit_bytes=63 * 1024 * 1024
+            collective_id=0, has_side_effects=True, vmem_limit_bytes=56 * 1024 * 1024
         ),
         name="test_time_step",
     )(

time: 106 us -> 97.5 us (0.920)
  Pallas kernels: 99.6 us -> 91.3 us
    pallas_call x1, Pallas kernels: 99.6 us -> 91.3 us  [fused_body(): pl.pallas_call(fused_kernel, out_shape=(jax.ShapeDtypeStruct((rank, part)...]
where the time goes in v1:
time: 97.5 us; the launch traced here: 97.1 us
  Pallas kernels  91.3 us (94%)
  local copies, waits for them, and re-layouts  5.11 us (5%)
    pallas_call x1, Pallas kernels, fused_body(): pl.pallas_call(fused_kernel, out_shape=(jax.ShapeDtypeStruct((rank, part)...  91.3 us
    unnamed x3, local copies, waits for them, and re-layouts  5.11 us

profile of v1, /device:TPU:1, one launch (start us, length us, event | category | flops | bytes accessed | tf_op | source)
XLA Modules:
  0.0 97.1 jit_solution(9885969908645494813)
XLA Ops:
  0.6 91.3 %test_time_step.1 = (f32[64,1024]{1,0:T(8,128)}, f32[64,512]{1,0:T(8,128)}, bf16[64,4096]{1,0:T(8,128)(2,1)}) custom-call(bf16[256,8192]{1,0:T(8,128)(2,1)} %bitcast.13, bf16[256,4096]{1,0:T(8,128)(2,1)} %bitcast.14, bf16[256,512]{1,0:T(8,128)(2,1)} %bitcast.20, bf16[256,4096]{1,0:T(8,128)(2,1)} %bitcast.15, s32[1,256]{1,0:T(1,128)} %bitcast.24, ...), custom_call_target="tpu_custom_call" | custom-call | tf_op jit(solution)/shard_map/test_time_step/pallas_call | solution.py:679
  92.0 1.7 %copy.18 = f32[1024,64]{0,1:T(8,128)} copy(f32[1024,64]{0,1:T(8,128)} %bitcast.22) | data formatting | bytes 524288
  93.6 1.6 %copy.19 = f32[64,512]{1,0:T(8,128)} copy(f32[64,512]{1,0:T(8,128)} %get-tuple-element.13) | data formatting | bytes 262144
  95.2 1.9 %copy.20 = bf16[1,64,4096]{2,1,0:T(8,128)(2,1)} copy(bf16[1,64,4096]{2,1,0:T(8,128)(2,1)} %bitcast.19) | data formatting | bytes 1048576

commit v2 on v1

--- a/solution.py
+++ b/solution.py
@@ -193,7 +193,7 @@
     xs, qs, ks, goal, seg, down_t, up_ref, sq, sk, sseg, seg_col, wbuf, dbuf, ndbuf, probs, sprobs, base, vals, dvals,
     low_s, slow_s, slow_recv, gsend, gpair, rsend, rside, rline, rrecv, fhalf, frecv,
     gu, gupair, gusum, guside, guline, guall,
-    s_loc, s_w, r_w, s_wc, r_wc, s_d, r_d, s_nd, r_nd, s_gp, r_gp, s_rx, r_rx, s_rs, r_rs, s_f, r_f,
+    s_loc, s_w, s_wz, r_w, s_wc, r_wc, s_d, s_dz, r_d, s_nd, r_nd, s_gp, r_gp, s_rx, r_rx, s_rs, r_rs, s_f, r_f,
     s_up, r_up, s_ur, r_ur, s_ua, r_ua, s_uc, r_uc, s_sx, r_sx, s_sl, r_sl,
 ):
     t, f, c = lax.axis_index("task"), lax.axis_index("fsdp"), lax.axis_index("view")
@@ -300,111 +300,89 @@
         dbuf[2 * f + side] = down_t[:, side * half:(side + 1) * half].astype(BF16)
     pl.semaphore_wait(barrier, N + 1)
 
-    line = [(d, s, z - s * d) for d in range(1, DEPTH) for s in (1, -1)]
-
-    def inside(zp):
-        return jnp.logical_and(zp >= 0, zp < DEPTH)
-
-    def piece_send(buf, s_sem, r_sem, kind, i, pred=True):
-        send(kind, buf.at[i], buf.at[i], s_sem.at[kind, i], r_sem.at[i], pred)
-
-    def pieces_own(buf, s_sem, r_sem):
-        for kind in (UP, DOWN, SIDE):
-            piece_send(buf, s_sem, r_sem, kind, 2 * f + c)
-
-    def pieces_line(buf, s_sem, r_sem, d):
-        for dd, s, zp in line:
-            if dd == d:
-                ok, i = inside(zp), 2 * (2 * zp + x) + c
-                arrived(buf.at[i], r_sem.at[i], ok)
-                for kind in (UP if s > 0 else DOWN, SIDE, CORE):
-                    piece_send(buf, s_sem, r_sem, kind, i, ok)
-
-    def pieces_side(buf, s_sem, r_sem, d):
-        for dd, s, zp in [(0, 1, z)] + line:
-            if dd == d:
-                ok, i = (True if d == 0 else inside(zp)), 2 * (2 * zp + other_x) + c
-                arrived(buf.at[i], r_sem.at[i], ok)
-                piece_send(buf, s_sem, r_sem, CORE, i, ok)
-
-    def pieces_core(buf, r_sem):
+    to_turn = [lax.rem(z + k, DEPTH) for k in range(1, DEPTH)]
+    from_turn = [lax.rem(z + DEPTH - k, DEPTH) for k in range(1, DEPTH)]
+
+    def d_own():
+        i = 2 * f + c
+        send(SIDE, dbuf.at[i], dbuf.at[i], s_d.at[SIDE, i], r_d.at[i])
+        for k, zt in enumerate(to_turn):
+            peer_send(2 * zt + x, dbuf.at[i], dbuf.at[i], s_dz.at[k], r_d.at[i])
+
+    def d_line(k):
+        i = 2 * (2 * from_turn[k] + x) + c
+        arrived(dbuf.at[i], r_d.at[i])
+        for kind in (SIDE, CORE):
+            send(kind, dbuf.at[i], dbuf.at[i], s_d.at[kind, i], r_d.at[i])
+
+    def d_side():
+        for zt in [z] + from_turn:
+            i = 2 * (2 * zt + other_x) + c
+            arrived(dbuf.at[i], r_d.at[i])
+            send(CORE, dbuf.at[i], dbuf.at[i], s_d.at[CORE, i], r_d.at[i])
+
+    def d_core():
         for peer in peers():
             i = 2 * peer + other_c
-            arrived(buf.at[i], r_sem.at[i])
+            arrived(dbuf.at[i], r_d.at[i])
 
     mine, theirs = 2 * c + t, 2 * c + other_t
 
     def w_send(h, kind, i, pred=True):
         send(kind, wbuf.at[h, i], wbuf.at[h, i], s_w.at[h, kind, i], r_w.at[h, i], pred)
 
-    def w_wait(h, i, pred=True):
-        arrived(wbuf.at[h, i], r_w.at[h, i], pred)
-
-    def w_core(h, shard, pred=True):
+    def w_wait(h, i):
+        arrived(wbuf.at[h, i], r_w.at[h, i])
+
+    def w_core(h, shard):
         pair = wbuf.at[h, pl.ds(4 * shard + 2 * c, 2)]
-        send(CORE, pair, pair, s_wc.at[h, shard], r_wc.at[h, shard], pred)
+        send(CORE, pair, pair, s_wc.at[h, shard], r_wc.at[h, shard])
 
     def w_own(h):
-        for kind, q in ((UP, mine), (DOWN, mine), (SIDE, mine), (SIDE, theirs)):
+        cols = pl.ds(h * wcols, wcols)
+        for q in (mine, theirs):
             i = 4 * f + q
-            src = w_hbm.at[q, :, pl.ds(h * wcols, wcols)]
-            send(kind, src, wbuf.at[h, i], s_w.at[h, kind, i], r_w.at[h, i])
-
-    def w_line(h, d):
-        for dd, s, zp in line:
-            if dd == d:
-                ok, i = inside(zp), 4 * (2 * zp + x) + mine
-                w_wait(h, i, ok)
-                for kind in (UP if s > 0 else DOWN, SIDE, TWIN):
-                    w_send(h, kind, i, ok)
-
-    def w_side(h, d):
-        if d == 0:
-            i = 4 * (2 * z + other_x) + mine
-            w_wait(h, i)
-            i = 4 * (2 * z + other_x) + theirs
-            w_wait(h, i)
-            for kind in (UP, DOWN):
-                w_send(h, kind, i)
-            w_core(h, 2 * z + other_x)
-            return
-        for dd, s, zp in line:
-            if dd == d:
-                ok, i = inside(zp), 4 * (2 * zp + other_x) + mine
-                w_wait(h, i, ok)
-                if d > 1:
-                    w_send(h, TWIN, i, ok)
-
-    def w_twin(h, d, xx):
-        for dd, s, zp in line:
-            if dd == d:
-                ok, i = inside(zp), 4 * (2 * zp + xx) + theirs
-                w_wait(h, i, ok)
-                w_core(h, 2 * zp + xx, ok)
-
-    def shards(d):
-        if d == 0:
-            return [(True, f), (True, 2 * z + other_x)]
-        return [(inside(zp), 2 * zp + xx) for dd, s, zp in line if dd == d for xx in (x, other_x)]
-
-    def run(pred, step):
-        if pred is True:
-            step()
-        else:
-            pl.when(pred)(step)
-
-    def add_base(h, d):
-        for n, (ok, shard) in enumerate(shards(d)):
-            def step(n=n, shard=shard):
-                if d or n:
-                    arrived(wbuf.at[h, pl.ds(4 * shard + 2 * other_c, 2)], r_wc.at[h, shard])
-                weight = wbuf[h, pl.ds(4 * shard, 4)].reshape(part, wcols)
-                both = xs[pl.ds(0, rows + BLOCK), lanes(shard * part, part)]
-                base[:, h * wcols:(h + 1) * wcols] += dot(both, weight)
-
-            run(ok, step)
-
-    def train_probs(b):
+            send(SIDE, w_hbm.at[q, :, cols], wbuf.at[h, i], s_w.at[h, SIDE, i], r_w.at[h, i])
+        i = 4 * f + mine
+        for k, zt in enumerate(to_turn):
+            peer_send(2 * zt + x, w_hbm.at[mine, :, cols], wbuf.at[h, i], s_wz.at[h, k], r_w.at[h, i])
+
+    def w_line(h, k):
+        i = 4 * (2 * from_turn[k] + x) + mine
+        w_wait(h, i)
+        for kind in (SIDE, TWIN):
+            w_send(h, kind, i)
+
+    def w_side_own(h):
+        shard = 2 * z + other_x
+        w_wait(h, 4 * shard + mine)
+        w_wait(h, 4 * shard + theirs)
+        for kind in (UP, DOWN):
+            w_send(h, kind, 4 * shard + theirs)
+        w_core(h, shard)
+
+    def w_side(h, k):
+        zt = from_turn[k]
+        i = 4 * (2 * zt + other_x) + mine
+        w_wait(h, i)
+        w_send(h, TWIN, i, jnp.logical_and(zt - z != 1, z - zt != 1))
+
+    def w_twin(h, k, xx):
+        shard = 2 * from_turn[k] + xx
+        w_wait(h, 4 * shard + theirs)
+        w_core(h, shard)
+
+    def add_base(h):
+        shards = [2 * zt + xx for zt in [z] + from_turn for xx in (x, other_x)]
+        for n, shard in enumerate(shards):
+            if n:
+                arrived(wbuf.at[h, pl.ds(4 * shard + 2 * other_c, 2)], r_wc.at[h, shard])
+            weight = wbuf[h, pl.ds(4 * shard, 4)].reshape(part, wcols)
+            both = xs[pl.ds(0, rows + BLOCK), lanes(shard * part, part)]
+            base[:, h * wcols:(h + 1) * wcols] += dot(both, weight)
+
+    def train_probs(step):
+        b, pair = step // 2, step % 2
         first = max(b - 1, 0) * BLOCK
         position_q = b * BLOCK + lax.broadcasted_iota(jnp.int32, (BLOCK, WINDOW), 0)
         position_k = first + lax.broadcasted_iota(jnp.int32, (BLOCK, WINDOW), 1)
@@ -417,7 +395,7 @@
             probs[b * KV_HEADS + g] = softmax_rows(nt_dot(q, k), allowed)
             return 0
 
-        lax.fori_loop(0, KV_HEADS, head_group, 0)
+        lax.fori_loop(pair * KV_HEADS // 2, (pair + 1) * KV_HEADS // 2, head_group, 0)
 
     def score_probs():
         order_q = lax.broadcasted_iota(jnp.int32, (BLOCK, BLOCK), 0)
@@ -455,8 +433,7 @@
             lax.fori_loop(h * KV_HEADS // 2, (h + 1) * KV_HEADS // 2, head_group, 0)
 
     sx_other = xs.at[pl.ds(rows + BLOCK, BLOCK)]
-    dset = (dbuf, s_d, r_d)
-    pieces_own(*dset)
+    d_own()
     w_own(0)
     base[...] = jnp.zeros_like(base)
     dvals[...] = jnp.zeros_like(dvals)
@@ -464,55 +441,53 @@
         loads[i].wait()
     seg_col[...] = jnp.broadcast_to(seg[...].astype(F32), (WINDOW, rows)).T
     train_probs(0)
-    pieces_line(*dset, 1)
+    w_side_own(0)
+    w_line(0, 0)
+    train_probs(1)
     w_line(0, 1)
-    pieces_side(*dset, 0)
-    w_side(0, 0)
     w_own(1)
     send(CORE, sx_hbm, sx_other, s_sx, r_sx)
-    train_probs(1)
-    pieces_line(*dset, 2)
+    train_probs(2)
     w_line(0, 2)
-    pieces_side(*dset, 1)
+    for k in range(DEPTH - 1):
+        d_line(k)
+    train_probs(3)
+    w_side(0, 0)
+    w_twin(0, 0, x)
+    train_probs(4)
+    w_side_own(1)
+    w_line(1, 0)
     w_side(0, 1)
     w_twin(0, 1, x)
-    w_twin(0, 1, other_x)
-    train_probs(2)
-    pieces_line(*dset, 3)
-    w_line(0, 3)
-    pieces_side(*dset, 2)
+    train_probs(5)
+    w_line(1, 1)
     w_side(0, 2)
     w_twin(0, 2, x)
-    w_line(1, 1)
+    train_probs(6)
+    w_line(1, 2)
+    d_side()
+    w_twin(0, 0, other_x)
+    w_twin(0, 1, other_x)
+    train_probs(7)
     w_side(1, 0)
-    train_probs(3)
-    pieces_side(*dset, 3)
-    w_side(0, 3)
-    w_twin(0, 2, other_x)
-    w_twin(0, 3, x)
-    w_line(1, 2)
-    w_side(1, 1)
+    w_twin(1, 0, x)
     for i in range(4, len(loads)):
         loads[i].wait()
     score_probs()
+    w_twin(0, 2, other_x)
+    w_side(1, 1)
     w_twin(1, 1, x)
-    w_twin(1, 1, other_x)
-    w_line(1, 3)
-    w_twin(0, 3, other_x)
-    pieces_core(dbuf, r_d)
+    d_core()
     low = lax.fori_loop(0, 2 * N, low_step, jnp.zeros((rows, low_s.shape[1]), F32)).astype(BF16)
     low_s[...] = low
     w_side(1, 2)
     w_twin(1, 2, x)
-    for d in range(DEPTH):
-        add_base(0, d)
-    w_side(1, 3)
+    add_base(0)
+    w_twin(1, 0, other_x)
+    w_twin(1, 1, other_x)
+    attention(0)
     w_twin(1, 2, other_x)
-    w_twin(1, 3, x)
-    attention(0)
-    w_twin(1, 3, other_x)
-    for d in range(DEPTH):
-        add_base(1, d)
+    add_base(1)
     attention(1)
     up_half = up_ref[...].astype(BF16)
     dv = dvals[...].astype(BF16)
@@ -521,7 +496,7 @@
     def grad_of(peer, side):
         return dot(dlow_t, xs[pl.ds(0, rows), lanes(peer * part + side * half, half)])
 
-    turns = [lax.rem(z + k, DEPTH) for k in range(1, DEPTH)] + [z]
+    turns = to_turn + [z]
     order = [2 * zt + xx for zt in turns for xx in (other_x, x)]
     for n, peer in enumerate(order):
         gsend[n] = grad_of(peer, other_c).astype(BF16)
@@ -571,12 +546,12 @@
     arrived(sx_other, r_sx)
     slow = slow_of(f)
     for k in range(DEPTH - 1):
-        shard = 2 * turns[k] + x
+        shard = 2 * from_turn[k] + x
         arrived(ndbuf.at[shard], r_nd.at[shard])
         send(SIDE, ndbuf.at[shard], ndbuf.at[shard], s_nd.at[DEPTH + k], r_nd.at[shard])
     for k in range(DEPTH - 1):
-        slow = slow + slow_of(2 * turns[k] + x)
-        arrived(guline.at[turns[k]], r_ua.at[turns[k]])
+        slow = slow + slow_of(2 * from_turn[k] + x)
+        arrived(guline.at[from_turn[k]], r_ua.at[from_turn[k]])
     utotal = guline[0].astype(F32)
     for k in range(1, DEPTH):
         utotal = utotal + guline[k].astype(F32)
@@ -585,7 +560,7 @@
     arrived(frecv, r_f)
     new_down_t[:, lanes(c * half, half)] = fhalf[...]
     new_down_t[:, lanes(other_c * half, half)] = frecv[...]
-    for zt in [z] + turns[:-1]:
+    for zt in [z] + from_turn:
         shard = 2 * zt + other_x
         arrived(ndbuf.at[shard], r_nd.at[shard])
         slow = slow + slow_of(shard)
@@ -607,6 +582,16 @@
             scored[:, at:at + HEAD_DIM] = attended[j * BLOCK:(j + 1) * BLOCK]
 
     flush()
+
+
+def hand_over(a, b, c, a_out, b_out, c_out, sems):
+    copies = [
+        pltpu.make_async_copy(src, dst, sems.at[i]) for i, (src, dst) in enumerate(((a, a_out), (b, b_out), (c, c_out)))
+    ]
+    for copy in copies:
+        copy.start()
+    for copy in copies:
+        copy.wait()
 
 
 def fused_body(
@@ -661,9 +646,9 @@
         pltpu.VMEM((DEPTH, rank, uc), BF16),
         pltpu.VMEM((2, rank, uc), F32),
         sem((13,)),
-        sem((2, 5, 4 * N)), sem((2, 4 * N)),
+        sem((2, 5, 4 * N)), sem((2, DEPTH - 1)), sem((2, 4 * N)),
         sem((2, N)), sem((2, N)),
-        sem((5, 2 * N)), sem((2 * N,)),
+        sem((5, 2 * N)), sem((DEPTH - 1,)), sem((2 * N,)),
         sem((2 * DEPTH - 1,)), sem((N,)),
         sem((N,)), sem((N,)),
         sem((DEPTH,)), sem((DEPTH,)),
@@ -695,6 +680,15 @@
         value_weight.reshape(4, part // 4, vw), adapter_down.T, adapter_up,
         score_input[0], score_query[0], score_keys[0], score_segments.reshape(1, srows),
     )
+    new_down_t, new_up, scored = pl.pallas_call(
+        hand_over,
+        out_shape=tuple(jax.ShapeDtypeStruct(a.shape, a.dtype) for a in (new_down_t, new_up, scored)),
+        in_specs=[hbm] * 3,
+        out_specs=(hbm,) * 3,
+        scratch_shapes=[sem((3,))],
+        compiler_params=pltpu.CompilerParams(vmem_limit_bytes=56 * 1024 * 1024),
+        name="hand_over",
+    )(new_down_t, new_up, scored)
     return (new_down_t.T, new_up, scored[None])
 
 

time: 97.5 us -> 127 us (1.30)
  Pallas kernels: 91.3 us -> 126 us
  local copies, waits for them, and re-layouts: 5.11 us -> 0 us
    pallas_call x0 -> x1, Pallas kernels: none -> 28.9 us  [fused_body(): pl.pallas_call(hand_over, out_shape=tuple((jax.ShapeDtypeStruct(a.shape,...]
    pallas_call x1, Pallas kernels: 91.3 us -> 96.8 us  [fused_body(): pl.pallas_call(fused_kernel, out_shape=(jax.ShapeDtypeStruct((rank, part)...]
    unnamed x3 -> x0, local copies, waits for them, and re-layouts: 5.11 us -> none
where the time goes in v2:
time: 127 us; the launch traced here: 126 us
  Pallas kernels  126 us (99%)
    pallas_call x1, Pallas kernels, fused_body(): pl.pallas_call(fused_kernel, out_shape=(jax.ShapeDtypeStruct((rank, part)...  96.8 us
    pallas_call x1, Pallas kernels, fused_body(): pl.pallas_call(hand_over, out_shape=tuple((jax.ShapeDtypeStruct(a.shape,...  28.9 us

profile of v2, /device:TPU:1, one launch (start us, length us, event | category | flops | bytes accessed | tf_op | source)
XLA Modules:
  0.0 126.4 jit_solution(8263007139725214620)
XLA Ops:
  0.6 96.8 %test_time_step.1 = (f32[64,1024]{1,0:T(8,128)}, f32[64,512]{1,0:T(8,128)}, bf16[64,4096]{1,0:T(8,128)(2,1)}) custom-call(bf16[256,8192]{1,0:T(8,128)(2,1)} %bitcast.13, bf16[256,4096]{1,0:T(8,128)(2,1)} %bitcast.14, bf16[256,512]{1,0:T(8,128)(2,1)} %bitcast.19, bf16[256,4096]{1,0:T(8,128)(2,1)} %bitcast.15, s32[1,256]{1,0:T(1,128)} %bitcast.22, ...), custom_call_target="tpu_custom_call" | custom-call | tf_op jit(solution)/shard_map/test_time_step/pallas_call | solution.py:664
  97.5 28.9 %hand_over.1 = (f32[64,1024]{1,0:T(8,128)}, f32[64,512]{1,0:T(8,128)}, bf16[64,4096]{1,0:T(8,128)(2,1)}) custom-call(f32[64,1024]{1,0:T(8,128)} %get-tuple-element.9.a, f32[64,512]{1,0:T(8,128)} %get-tuple-element.10.b, bf16[64,4096]{1,0:T(8,128)(2,1)} %get-tuple-element.11.c), custom_call_target="tpu_custom_call" | custom-call | tf_op jit(solution)/shard_map/hand_over/pallas_call | solution.py:683

commit v3 on v1

--- a/solution.py
+++ b/solution.py
@@ -279,19 +279,20 @@
     for kind in (TWIN, CORE):
         pl.semaphore_signal(barrier, inc=1, device_id=device(kind), device_id_type=pl.DeviceIdType.MESH)
 
-    local = [
-        (down_hbm, down_t),
+    local = [(down_hbm, down_t)]
+    local += [(w_hbm.at[:, :, pl.ds(h * wcols, wcols)], wbuf.at[h, pl.ds(4 * f, 4)]) for h in range(2)]
+    local += [
         (q_hbm, qs),
         (k_hbm, ks),
         (seg_hbm, seg),
+        (sx_hbm, xs.at[pl.ds(rows, BLOCK)]),
         (sq_hbm, sq),
         (sk_hbm, sk),
         (sseg_hbm, sseg),
         (x_hbm, xs.at[pl.ds(0, rows)]),
-        (sx_hbm, xs.at[pl.ds(rows, BLOCK)]),
         (up_hbm, up_ref),
         (goal_hbm, goal),
-    ] + [(w_hbm.at[:, :, pl.ds(h * wcols, wcols)], wbuf.at[h, pl.ds(4 * f, 4)]) for h in range(2)]
+    ]
     loads = [pltpu.make_async_copy(a, b, s_loc.at[i]) for i, (a, b) in enumerate(local)]
     for load in loads:
         load.start()
@@ -347,8 +348,7 @@
     def w_own(h):
         for kind, q in ((UP, mine), (DOWN, mine), (SIDE, mine), (SIDE, theirs)):
             i = 4 * f + q
-            src = w_hbm.at[q, :, pl.ds(h * wcols, wcols)]
-            send(kind, src, wbuf.at[h, i], s_w.at[h, kind, i], r_w.at[h, i])
+            w_send(h, kind, i)
 
     def w_line(h, d):
         for dd, s, zp in line:
@@ -404,7 +404,8 @@
 
             run(ok, step)
 
-    def train_probs(b):
+    def train_probs(step):
+        b, pair = step // 2, step % 2
         first = max(b - 1, 0) * BLOCK
         position_q = b * BLOCK + lax.broadcasted_iota(jnp.int32, (BLOCK, WINDOW), 0)
         position_k = first + lax.broadcasted_iota(jnp.int32, (BLOCK, WINDOW), 1)
@@ -417,7 +418,7 @@
             probs[b * KV_HEADS + g] = softmax_rows(nt_dot(q, k), allowed)
             return 0
 
-        lax.fori_loop(0, KV_HEADS, head_group, 0)
+        lax.fori_loop(pair * KV_HEADS // 2, (pair + 1) * KV_HEADS // 2, head_group, 0)
 
     def score_probs():
         order_q = lax.broadcasted_iota(jnp.int32, (BLOCK, BLOCK), 0)
@@ -457,47 +458,54 @@
     sx_other = xs.at[pl.ds(rows + BLOCK, BLOCK)]
     dset = (dbuf, s_d, r_d)
     pieces_own(*dset)
+    loads[1].wait()
     w_own(0)
     base[...] = jnp.zeros_like(base)
     dvals[...] = jnp.zeros_like(dvals)
-    for i in range(1, 4):
+    for i in range(3, 6):
         loads[i].wait()
     seg_col[...] = jnp.broadcast_to(seg[...].astype(F32), (WINDOW, rows)).T
     train_probs(0)
     pieces_line(*dset, 1)
     w_line(0, 1)
+    w_side(0, 0)
+    loads[2].wait()
+    w_own(1)
     pieces_side(*dset, 0)
-    w_side(0, 0)
-    w_own(1)
-    send(CORE, sx_hbm, sx_other, s_sx, r_sx)
+    loads[6].wait()
+    send(CORE, xs.at[pl.ds(rows, BLOCK)], sx_other, s_sx, r_sx)
     train_probs(1)
     pieces_line(*dset, 2)
     w_line(0, 2)
+    train_probs(2)
+    w_side(0, 1)
     pieces_side(*dset, 1)
-    w_side(0, 1)
     w_twin(0, 1, x)
-    w_twin(0, 1, other_x)
-    train_probs(2)
     pieces_line(*dset, 3)
     w_line(0, 3)
+    train_probs(3)
+    w_line(1, 1)
+    w_side(1, 0)
+    w_twin(0, 1, other_x)
     pieces_side(*dset, 2)
+    train_probs(4)
     w_side(0, 2)
     w_twin(0, 2, x)
-    w_line(1, 1)
-    w_side(1, 0)
-    train_probs(3)
+    w_line(1, 2)
+    train_probs(5)
     pieces_side(*dset, 3)
     w_side(0, 3)
+    w_twin(0, 3, x)
+    train_probs(6)
+    w_side(1, 1)
+    w_line(1, 3)
     w_twin(0, 2, other_x)
-    w_twin(0, 3, x)
-    w_line(1, 2)
-    w_side(1, 1)
-    for i in range(4, len(loads)):
+    train_probs(7)
+    w_twin(1, 1, x)
+    w_twin(1, 1, other_x)
+    for i in range(7, len(loads)):
         loads[i].wait()
     score_probs()
-    w_twin(1, 1, x)
-    w_twin(1, 1, other_x)
-    w_line(1, 3)
     w_twin(0, 3, other_x)
     pieces_core(dbuf, r_d)
     low = lax.fori_loop(0, 2 * N, low_step, jnp.zeros((rows, low_s.shape[1]), F32)).astype(BF16)
@@ -607,6 +615,21 @@
             scored[:, at:at + HEAD_DIM] = attended[j * BLOCK:(j + 1) * BLOCK]
 
     flush()
+
+
+def hand_over(a, b, c, a_out, b_out, c_out, a_here, b_here, c_here, s_in, s_out):
+    here = (a_here, b_here, c_here)
+    loads = [pltpu.make_async_copy(src, dst, s_in.at[i]) for i, (src, dst) in enumerate(zip((a, b, c), here))]
+    stores = [
+        pltpu.make_async_copy(src, dst, s_out.at[i]) for i, (src, dst) in enumerate(zip(here, (a_out, b_out, c_out)))
+    ]
+    for load in loads:
+        load.start()
+    for load, store in zip(loads, stores):
+        load.wait()
+        store.start()
+    for store in stores:
+        store.wait()
 
 
 def fused_body(
@@ -695,6 +718,17 @@
         value_weight.reshape(4, part // 4, vw), adapter_down.T, adapter_up,
         score_input[0], score_query[0], score_keys[0], score_segments.reshape(1, srows),
     )
+    results = (new_down_t, new_up, scored)
+    shapes = [(a.shape, a.dtype) for a in results]
+    new_down_t, new_up, scored = pl.pallas_call(
+        hand_over,
+        out_shape=tuple(jax.ShapeDtypeStruct(*a) for a in shapes),
+        in_specs=[hbm] * 3,
+        out_specs=(hbm,) * 3,
+        scratch_shapes=[*(pltpu.VMEM(*a) for a in shapes), sem((3,)), sem((3,))],
+        compiler_params=pltpu.CompilerParams(vmem_limit_bytes=56 * 1024 * 1024),
+        name="hand_over",
+    )(*results)
     return (new_down_t.T, new_up, scored[None])
 
 

time: 97.5 us -> 93.8 us (0.962)
  local copies, waits for them, and re-layouts: 5.11 us -> 0 us
  Pallas kernels: 91.3 us -> 92.5 us
    unnamed x3 -> x0, local copies, waits for them, and re-layouts: 5.11 us -> none
    pallas_call x0 -> x1, Pallas kernels: none -> 2.03 us  [fused_body(): pl.pallas_call(hand_over, out_shape=tuple((jax.ShapeDtypeStruct(*a) for a...]
where the time goes in v3:
time: 93.8 us; the launch traced here: 93.4 us
  Pallas kernels  92.5 us (99%)
    pallas_call x1, Pallas kernels, fused_body(): pl.pallas_call(fused_kernel, out_shape=(jax.ShapeDtypeStruct((rank, part)...  90.5 us
    pallas_call x1, Pallas kernels, fused_body(): pl.pallas_call(hand_over, out_shape=tuple((jax.ShapeDtypeStruct(*a) for a...  2.03 us

profile of v3, /device:TPU:1, one launch (start us, length us, event | category | flops | bytes accessed | tf_op | source)
XLA Modules:
  0.0 93.4 jit_solution(17032470098495761836)
XLA Ops:
  0.6 90.5 %test_time_step.1 = (f32[64,1024]{1,0:T(8,128)}, f32[64,512]{1,0:T(8,128)}, bf16[64,4096]{1,0:T(8,128)(2,1)}) custom-call(bf16[256,8192]{1,0:T(8,128)(2,1)} %bitcast.13, bf16[256,4096]{1,0:T(8,128)(2,1)} %bitcast.14, bf16[256,512]{1,0:T(8,128)(2,1)} %bitcast.19, bf16[256,4096]{1,0:T(8,128)(2,1)} %bitcast.15, s32[1,256]{1,0:T(1,128)} %bitcast.22, ...), custom_call_target="tpu_custom_call" | custom-call | tf_op jit(solution)/shard_map/test_time_step/pallas_call | solution.py:702
  91.2 2.0 %hand_over.1 = (f32[64,1024]{1,0:T(8,128)}, f32[64,512]{1,0:T(8,128)}, bf16[64,4096]{1,0:T(8,128)(2,1)}) custom-call(f32[64,1024]{1,0:T(8,128)} %get-tuple-element.9.a, f32[64,512]{1,0:T(8,128)} %get-tuple-element.10.b, bf16[64,4096]{1,0:T(8,128)(2,1)} %get-tuple-element.11.c), custom_call_target="tpu_custom_call" | custom-call | tf_op jit(solution)/shard_map/hand_over/pallas_call | solution.py:723

commit v4 on v3

--- a/solution.py
+++ b/solution.py
@@ -259,16 +259,16 @@
         else:
             pl.when(pred)(wait)
 
-    def flush():
+    def flush(count):
         def finish(make):
             make().wait_send()
 
-        for make, pred in late:
+        for make, pred in late[:count]:
             if pred is True:
                 finish(make)
             else:
                 pl.when(pred)(lambda make=make: finish(make))
-        late.clear()
+        del late[:count]
 
     def peers():
         return [lax.rem(f + k, N) for k in range(1, N)]
@@ -531,12 +531,11 @@
 
     turns = [lax.rem(z + k, DEPTH) for k in range(1, DEPTH)] + [z]
     order = [2 * zt + xx for zt in turns for xx in (other_x, x)]
-    for n, peer in enumerate(order):
-        gsend[n] = grad_of(peer, other_c).astype(BF16)
+    older = len(late)
+
+    def to_core(n):
+        gsend[n] = grad_of(order[n], other_c).astype(BF16)
         send(CORE, gsend.at[n], gpair.at[n], s_gp.at[n], r_gp.at[n])
-    gu[...] = adapter_scale_factor * tn_dot(low_s[...], dv)
-    ucols = VALUE_WIDTH // 2
-    send(CORE, gu.at[:, lanes(other_c * ucols, ucols)], gupair, s_up, r_up)
 
     def core_sum(n):
         mine_of = grad_of(order[n], c)
@@ -544,11 +543,14 @@
         return mine_of + gpair[n].astype(F32)
 
     for k in range(DEPTH):
+        to_core(2 * k)
+    for k in range(DEPTH):
+        to_core(2 * k + 1)
         rsend[k] = core_sum(2 * k).astype(BF16)
         send(SIDE, rsend.at[k], rside.at[k], s_rx.at[k], r_rx.at[k])
-    arrived(gupair, r_up)
-    gusum[...] = gu[:, lanes(c * ucols, ucols)] + gupair[...]
-    send(SIDE, gusum, guside, s_ur, r_ur)
+    ucols = VALUE_WIDTH // 2
+    gu[...] = adapter_scale_factor * tn_dot(low_s[...], dv)
+    send(CORE, gu.at[:, lanes(other_c * ucols, ucols)], gupair, s_up, r_up)
     for k in range(DEPTH):
         total = core_sum(2 * k + 1)
         arrived(rside.at[k], r_rx.at[k])
@@ -556,9 +558,10 @@
         if k < DEPTH - 1:
             rline[k] = total.astype(BF16)
             peer_send(2 * turns[k] + x, rline.at[k], rrecv.at[k], s_rs.at[k], r_rs.at[k])
-    arrived(guside, r_ur)
-    guline[z] = (gusum[...] + guside[...]).astype(BF16)
-    flush()
+    arrived(gupair, r_up)
+    gusum[...] = gu[:, lanes(c * ucols, ucols)] + gupair[...]
+    send(SIDE, gusum, guside, s_ur, r_ur)
+    flush(older)
     for k in range(DEPTH - 1):
         arrived(rrecv.at[k], r_rs.at[k])
         total = total + rrecv[k].astype(F32)
@@ -567,6 +570,8 @@
     for k in range(DEPTH - 1):
         peer_send(2 * turns[k] + x, ndbuf.at[f], ndbuf.at[f], s_nd.at[k], r_nd.at[f])
     send(SIDE, ndbuf.at[f], ndbuf.at[f], s_nd.at[DEPTH - 1], r_nd.at[f])
+    arrived(guside, r_ur)
+    guline[z] = (gusum[...] + guside[...]).astype(BF16)
     for k in range(DEPTH - 1):
         peer_send(2 * turns[k] + x, guline.at[z], guline.at[z], s_ua.at[k], r_ua.at[z])
     fhalf[...] = new_half
@@ -614,7 +619,7 @@
             at = (g * GROUP + j) * HEAD_DIM
             scored[:, at:at + HEAD_DIM] = attended[j * BLOCK:(j + 1) * BLOCK]
 
-    flush()
+    flush(len(late))
 
 
 def hand_over(a, b, c, a_out, b_out, c_out, a_here, b_here, c_here, s_in, s_out):

time: 93.8 us -> 95 us (1.013)
  Pallas kernels: 92.5 us -> 94 us
    pallas_call x1, Pallas kernels: 90.5 us -> 92 us  [fused_body(): pl.pallas_call(fused_kernel, out_shape=(jax.ShapeDtypeStruct((rank, part)...]
where the time goes in v4:
time: 95 us; the launch traced here: 94.8 us
  Pallas kernels  94 us (99%)
    pallas_call x1, Pallas kernels, fused_body(): pl.pallas_call(fused_kernel, out_shape=(jax.ShapeDtypeStruct((rank, part)...  92 us
    pallas_call x1, Pallas kernels, fused_body(): pl.pallas_call(hand_over, out_shape=tuple((jax.ShapeDtypeStruct(*a) for a...  2.03 us

profile of v4, /device:TPU:1, one launch (start us, length us, event | category | flops | bytes accessed | tf_op | source)
XLA Modules:
  0.0 94.8 jit_solution(270277278676926999)
XLA Ops:
  0.6 92.0 %test_time_step.1 = (f32[64,1024]{1,0:T(8,128)}, f32[64,512]{1,0:T(8,128)}, bf16[64,4096]{1,0:T(8,128)(2,1)}) custom-call(bf16[256,8192]{1,0:T(8,128)(2,1)} %bitcast.13, bf16[256,4096]{1,0:T(8,128)(2,1)} %bitcast.14, bf16[256,512]{1,0:T(8,128)(2,1)} %bitcast.19, bf16[256,4096]{1,0:T(8,128)(2,1)} %bitcast.15, s32[1,256]{1,0:T(1,128)} %bitcast.22, ...), custom_call_target="tpu_custom_call" | custom-call | tf_op jit(solution)/shard_map/test_time_step/pallas_call | solution.py:707
  92.6 2.0 %hand_over.1 = (f32[64,1024]{1,0:T(8,128)}, f32[64,512]{1,0:T(8,128)}, bf16[64,4096]{1,0:T(8,128)(2,1)}) custom-call(f32[64,1024]{1,0:T(8,128)} %get-tuple-element.9.a, f32[64,512]{1,0:T(8,128)} %get-tuple-element.10.b, bf16[64,4096]{1,0:T(8,128)(2,1)} %get-tuple-element.11.c), custom_call_target="tpu_custom_call" | custom-call | tf_op jit(solution)/shard_map/hand_over/pallas_call | solution.py:728
